TPU v7x, 512 devices: a whole 4x4x16 slice. The times are simulated.
512 devices in a mesh: section: 32 (over x, z_lo), dp: 16 (over z_hi, y, core).
Axes of the slice: x: 4, y: 4, z: 16 (z_hi: 2, z_lo: 8; z = z_hi * 8 + z_lo), core: 2. Of those that a mesh axis runs over, the one named last changes fastest.
Arguments:
- memory: bfloat16 [2048, 2048], P('dp', 'section'), may hold values from -6 to 6
- queries: bfloat16 [32, 2048, 2048], P('section', 'dp'), may hold values from -6 to 6
- values: bfloat16 [32, 2048, 2048], P('section', 'dp'), may hold values from -6 to 6
- out_grad: bfloat16 [32, 2048, 2048], P('section', 'dp'), may hold values from -6 to 6
- key_weight: bfloat16 [32, 2048, 2048], P('section', 'dp'), may hold values from -0.125 to 0.125
- first_codes: bfloat16 [32, 2048, 2048], P('section', 'dp'), may hold values from -1 to 1
- first_scales: float32 [32, 16, 2048], P('section', None, 'dp'), may hold values from 0.5 to 5
- second_codes: bfloat16 [32, 2048, 2048], P('section', 'dp'), may hold values from 0.049804688 to 1
- second_scales: float32 [32, 16, 2048], P('section', None, 'dp'), may hold values from 2 to 20
Outputs:
- memory_grad: float32 [2048, 2048], P('dp', 'section')
- update: bfloat16 [32, 2048, 2048], P('section', 'dp')
- new_first_codes: bfloat16 [32, 2048, 2048], P('section', 'dp')
- new_first_scales: float32 [32, 16, 2048], P('section', None, 'dp')
- new_second_codes: bfloat16 [32, 2048, 2048], P('section', 'dp')
- new_second_scales: float32 [32, 16, 2048], P('section', None, 'dp')
All inputs are finite; a program needn't handle non-finite values. Where the computation divides by a largest or mean magnitude, that divisor is 1e-20 or more.
Results may differ from a plain program's by a relative error of at most 0.012.
Values may be sent and summed in bfloat16 or wider, within the bound.
A program may use at most 64 MiB of HBM per device.

v0:
```python
import jax
import jax.numpy as jnp
from jax import lax
from jax.sharding import PartitionSpec as P

HEADS = 8
HD = 256


beta_one = 0.9
beta_two = 0.95
corr_one = 1.0 - 0.9**10
corr_two = 1.0 - 0.95**10


def key_gradient(key_rows, queries, values, out_grad):
    scale = HD ** (-0.5)
    key_count = key_rows.shape[0]
    query_count = queries.shape[0]
    key_heads = key_rows.reshape(key_count, HEADS, HD)
    query_heads = queries.reshape(query_count, HEADS, HD)
    value_heads = values.reshape(key_count, HEADS, HD)
    grad_heads = out_grad.reshape(query_count, HEADS, HD)
    scores = (
        jnp.einsum("khd,qhd->hkq", key_heads, query_heads, preferred_element_type=jnp.float32)
        * scale
    )
    expon = jnp.exp(scores)
    probs = expon / jnp.sum(expon, axis=1, keepdims=True)
    prob_grad = jnp.einsum(
        "khd,qhd->hkq", value_heads, grad_heads, preferred_element_type=jnp.float32
    )
    score_grad = (
        probs * (prob_grad - jnp.sum(probs * prob_grad, axis=1, keepdims=True)) * scale
    ).astype(jnp.bfloat16)
    key_grad = jnp.einsum(
        "hkq,qhd->khd", score_grad, query_heads, preferred_element_type=jnp.float32
    )
    return key_grad.reshape(key_count, HEADS * HD).astype(jnp.bfloat16)


def adam_step(weight_grad, first_codes, first_scales, second_codes, second_scales):
    row_count = weight_grad.shape[0]
    blocks = first_scales.shape[0]
    first_prev = (
        first_codes.astype(jnp.float32).reshape(row_count, blocks, -1) * first_scales.T[:, :, None]
    )
    second_prev = (
        second_codes.astype(jnp.float32).reshape(row_count, blocks, -1)
        * second_scales.T[:, :, None]
    )
    grad_blocks = weight_grad.reshape(row_count, blocks, -1)
    first = beta_one * first_prev + (1.0 - beta_one) * grad_blocks
    second = beta_two * second_prev + (1.0 - beta_two) * grad_blocks * grad_blocks
    update = first / corr_one / (jnp.sqrt(second / corr_two) + 1e-08)
    first_max = jnp.max(jnp.abs(first), axis=2) + 1e-06
    second_max = jnp.max(second, axis=2) + 1e-06
    first_new = (first / first_max[:, :, None]).astype(jnp.bfloat16)
    second_new = (second / second_max[:, :, None]).astype(jnp.bfloat16)
    return (
        update.reshape(row_count, -1).astype(jnp.bfloat16),
        first_new.reshape(row_count, -1),
        first_max.T,
        second_new.reshape(row_count, -1),
        second_max.T,
    )


def local(
    memory,
    queries,
    values,
    out_grad,
    key_weight,
    first_codes,
    first_scales,
    second_codes,
    second_scales,
):
    encoded = lax.all_gather(memory, "section", axis=1, tiled=True)
    weight_local = key_weight[0]
    weight_full = lax.all_gather(weight_local, "dp", axis=0, tiled=True)
    key_rows = jnp.dot(encoded, weight_full, preferred_element_type=jnp.float32).astype(
        jnp.bfloat16
    )
    key_grad = key_gradient(key_rows, queries[0], values[0], out_grad[0])
    memory_term = lax.dot_general(
        key_grad, weight_full, (((1,), (1,)), ((), ())), preferred_element_type=jnp.float32
    )
    memory_grad = lax.psum_scatter(memory_term, "section", scatter_dimension=1, tiled=True)
    encoder_rows = lax.all_to_all(encoded, "dp", split_axis=1, concat_axis=0, tiled=True)
    weight_grad = lax.dot_general(
        encoder_rows,
        lax.all_gather(key_grad, "dp", axis=0, tiled=True),
        (((0,), (0,)), ((), ())),
        preferred_element_type=jnp.float32,
    )
    update, first_new, first_max, second_new, second_max = adam_step(
        weight_grad, first_codes[0], first_scales[0], second_codes[0], second_scales[0]
    )
    return (
        memory_grad,
        update[None],
        first_new[None],
        first_max[None],
        second_new[None],
        second_max[None],
    )


def solution(mesh):
    return jax.shard_map(
        local,
        mesh=mesh,
        in_specs=(
            P("dp", "section"),
            P("section", "dp", None),
            P("section", "dp", None),
            P("section", "dp", None),
            P("section", "dp", None),
            P("section", "dp", None),
            P("section", None, "dp"),
            P("section", "dp", None),
            P("section", None, "dp"),
        ),
        out_specs=(
            P("dp", "section"),
            P("section", "dp", None),
            P("section", "dp", None),
            P("section", None, "dp"),
            P("section", "dp", None),
            P("section", None, "dp"),
        ),
        check_vma=False,
    )
```

profile of v0, /device:TPU:16, one launch (start us, length us, event | category | flops | bytes accessed | tf_op | source)
XLA Modules:
  0.0 649.9 jit_solution(9433837871899278780)
XLA Ops:
  7.2 0.0 all-gather.6.cloned.1.call-start
  7.2 0.7 all-gather.6.cloned.1.call-update
  7.9 0.0 all-gather.4.cloned.1.call-start
  7.9 1.2 copy.49
  9.1 1.2 copy.51
  10.3 1.2 copy.50
  11.4 185.6 %all_gather.9 = bf16[128,2048]{0,1:T(8,128)(2,1)} all-gather(bf16[128,64]{0,1:T(8,128)(2,1)} %param.9), channel_id=1, replica_groups=mesh['section'=32,'dp'=16] {'section'}, dimensions={1}, use_global_device_ids=true | all-gather | bytes 540672 | tf_op jit(solution)/shard_map/all_gather | solution.py:80
  197.0 0.3 fusion.34
  197.4 2.3 all-gather.6.cloned.1.call-done
  199.7 4.8 fusion.6
  204.5 0.3 fusion.9
  204.9 0.0 copy-start
  204.9 0.0 copy-start.1
  204.9 0.4 fusion.10
  205.3 1.0 copy.41
  206.3 0.0 copy-start.2
  206.3 0.0 copy-start.3
  206.3 0.0 all-gather.4.cloned.1.call-update
  206.3 21.3 %all-to-all-start = ((bf16[128,16,128]{0,2,1:T(8,128)(2,1)}), bf16[128,16,128]{0,2,1:T(8,128)(2,1)S(1)}, u32[]{:S(2)}, u32[]{:S(2)}) async-start(bf16[128,16,128]{0,2,1:T(8,128)(2,1)} %bitcast.7), calls=%async_computation.1 | async-start | bytes 1048576 | tf_op jit(solution)/shard_map/all_to_all | solution.py:91
  227.6 0.0 reduce-scatter.2.cloned.1.call-start
  227.7 7.2 %fusion.2 = f32[128,2048]{0,1:T(8,128)} fusion(bf16[128,2048]{0,1:T(8,128)(2,1)} %bitcast.137, bf16[1,2048,2048]{2,1,0:T(8,128)(2,1)} %all-gather.6.cloned.1.call-done), kind=kOutput, calls=%fused_computation.2 | convolution fusion | flops 1073741824 | bytes 9961472 | tf_op jit(solution)/shard_map/dot_general | solution.py:87
  234.9 0.0 reduce-scatter.2.cloned.1.call-update
  234.9 0.0 copy-done
  235.0 0.3 copy.44
  235.2 0.0 copy-done.1
  235.2 0.3 copy.42
  235.5 33.2 %all-to-all-done = bf16[128,16,128]{0,2,1:T(8,128)(2,1)S(1)} async-done(((bf16[128,16,128]{0,2,1:T(8,128)(2,1)}), bf16[128,16,128]{0,2,1:T(8,128)(2,1)S(1)}, u32[]{:S(2)}, u32[]{:S(2)}) %all-to-all-start) | async-done | bytes 524320 | tf_op jit(solution)/shard_map/all_to_all | solution.py:91
  268.7 0.3 copy.43
  269.0 135.9 %all-gather.4.cloned.1.call-done = bf16[2048,2048]{0,1:T(8,128)(2,1)} async-done(((bf16[128,2048]{0,1:T(8,128)(2,1)}), bf16[2048,2048]{0,1:T(8,128)(2,1)}) %all-gather.4.cloned.1.call-update) | async-done | bytes 8388624 | tf_op jit(solution)/shard_map/all_gather | solution.py:94
  404.9 0.0 copy-done.2
  404.9 0.0 copy-done.3
  404.9 6.3 fusion.31
  411.2 1.0 copy.45
  412.2 0.6 fusion.17
  412.8 0.6 fusion.44
  413.4 0.5 fusion.18
  413.9 1.0 copy.46
  414.9 1.0 copy.47
  415.9 227.4 %reduce-scatter.2.cloned.1.call-done = f32[128,64]{0,1:T(8,128)} async-done(((f32[128,2048]{0,1:T(8,128)}), f32[128,64]{0,1:T(8,128)}) %reduce-scatter.2.cloned.1.call-update) | async-done | bytes 32784 | tf_op jit(solution)/shard_map/reduce_scatter | solution.py:90
Async XLA Ops:
  7.2 192.5 %all-gather.6.cloned.1.call-start = ((), (), s32[]{:S(2)}) async-start(), calls=%async_computation.4 | async-start | bytes 8912896 | tf_op jit(solution)/shard_map/all_gather | solution.py:82
  7.9 397.0 %all-gather.4.cloned.1.call-start = ((), (), s32[]{:S(2)}) async-start(), calls=%async_computation.3 | async-start | bytes 8912896 | tf_op jit(solution)/shard_map/all_gather | solution.py:94
  204.9 30.1 %copy-start = (bf16[1,128,2048]{2,1,0:T(8,128)(2,1)S(1)}, bf16[1,128,2048]{2,1,0:T(8,128)(2,1)}, u32[]{:S(2)}) copy-start(bf16[1,128,2048]{2,1,0:T(8,128)(2,1)} %param.16) | copy-start | bytes 1572868
  204.9 30.3 %copy-start.1 = (bf16[1,128,2048]{2,1,0:T(8,128)(2,1)S(1)}, bf16[1,128,2048]{2,1,0:T(8,128)(2,1)}, u32[]{:S(2)}) copy-start(bf16[1,128,2048]{2,1,0:T(8,128)(2,1)} %param.14) | copy-start | bytes 1572868
  206.3 198.6 %copy-start.2 = (f32[1,16,128]{2,1,0:T(8,128)S(1)}, f32[1,16,128]{2,1,0:T(8,128)}, u32[]{:S(2)}) copy-start(f32[1,16,128]{2,1,0:T(8,128)} %param.17) | copy-start | bytes 24580
  206.3 198.6 %copy-start.3 = (f32[1,16,128]{2,1,0:T(8,128)S(1)}, f32[1,16,128]{2,1,0:T(8,128)}, u32[]{:S(2)}) copy-start(f32[1,16,128]{2,1,0:T(8,128)} %param.15) | copy-start | bytes 24580
  206.3 62.3 %all-to-all-start = ((bf16[128,16,128]{0,2,1:T(8,128)(2,1)}), bf16[128,16,128]{0,2,1:T(8,128)(2,1)S(1)}, u32[]{:S(2)}, u32[]{:S(2)}) async-start(bf16[128,16,128]{0,2,1:T(8,128)(2,1)} %bitcast.7), calls=%async_computation.1 | async-start | bytes 1048576 | tf_op jit(solution)/shard_map/all_to_all | solution.py:91
  227.6 415.7 %reduce-scatter.2.cloned.1.call-start = ((), (), s32[]{:S(2)}) async-start(), calls=%async_computation.2 | async-start | bytes 1081344 | tf_op jit(solution)/shard_map/reduce_scatter | solution.py:90
Sparse Core Ops, SparseCore 0:
  11.3 188.3 all-gather.5
  206.5 198.4 all-gather.3
  408.3 235.0 reduce-scatter.1
where the time goes:
time: 650 us
  waiting for transfers between devices  400 us (62%)
  blocking collectives  186 us (29%)
  starting transfers between devices  21.4 us (3%)
  matrix products  19.4 us (3%)
  between operations  13.9 us (2%)
  local copies, waits for them, and re-layouts  8.32 us (1%)
    reduce_scatter x1, waiting for transfers between devices, local(): lax.psum_scatter(memory_term, 'section', scatter_dimension=1, tiled=True)  227 us
    all_gather x1, blocking collectives, local(): encoded = lax.all_gather(memory, 'section', axis=1, tiled=True)  186 us
    all_gather x1, waiting for transfers between devices, local(): lax.all_gather(key_grad, 'dp', axis=0, tiled=True)  136 us
    all_to_all x1, waiting for transfers between devices, local(): lax.all_to_all(encoded, 'dp', split_axis=1, concat_axis=0, tiled=True)  33.2 us
    all_to_all x1, starting transfers between devices, local(): lax.all_to_all(encoded, 'dp', split_axis=1, concat_axis=0, tiled=True)  21.3 us
  transfers between devices with their start and end apart: 4, of which 4 were waited for; matrix products, arithmetic and copies ran while one was open for 4% of the time, Pallas kernels for 0%

commit v1 on v0

v1 whole, which is shorter than its diff:
```python
import functools

import jax
import jax.numpy as jnp
from jax import lax
from jax.experimental import pallas as pl
from jax.experimental.pallas import tpu as pltpu
from jax.sharding import PartitionSpec as P

HEADS = 8
HD = 256
SCALE = HD ** (-0.5)
MESH = pl.DeviceIdType.MESH

beta_one = 0.9
beta_two = 0.95
corr_one = 1.0 - 0.9**10
corr_two = 1.0 - 0.95**10

GRAD_LAG = 8
NT = (((1,), (1,)), ((), ()))
NN = (((1,), (0,)), ((), ()))


def dot(a, b, dims=NN):
    return lax.dot_general(a, b, dims, preferred_element_type=jnp.float32)


def block_place(q):
    return (q % 2) * 8 + (q // 8) * 4 + (q // 2) % 4


def rows(start, size):
    return pl.ds(pl.multiple_of(start, size), size)


def wait_bytes(ref, sem):
    pltpu.make_async_copy(ref, ref, sem).wait()


def kernel(
    memory_ref, queries_ref, values_ref, out_grad_ref, weight_ref,
    codes_one_ref, scales_one_ref, codes_two_ref, scales_two_ref,
    memory_grad_ref, update_ref, new_one_ref, new_scale_one_ref, new_two_ref, new_scale_two_ref,
    weights, grads, slots, feats, encoded, feat_rows, terms, halves_out, halves_in, parts_out, parts_in,
    scale_cols_one, scale_cols_two, new_cols_one, new_cols_two,
    small_send, small_recv, w_send, w_z, w_y, w_core, g_send, g_z, g_y, g_core,
):
    s = lax.axis_index("section")
    q = lax.axis_index("dp")
    x, zl = lax.div(s, 8), lax.rem(s, 8)
    zh, y, core = lax.div(q, 8), lax.rem(lax.div(q, 2), 4), lax.rem(q, 2)

    far = (s, lax.rem(q + 8, 16))
    sibling = (s, q + 1 - 2 * core)
    along_y = [(s, zh * 8 + lax.rem(y + k, 4) * 2 + core) for k in (1, 3, 2)]
    along_x = [(lax.rem(s + 8 * k, 32), q) for k in (1, 3, 2)]
    along_z = [(x * 8 + lax.rem(zl + k, 8), q) for k in range(1, 8)]
    turn_to = (lax.rem(2 * q + lax.rem(s, 2) + 8, 32), lax.div(s, 2))
    turn_from = (2 * q + lax.rem(s, 2), lax.div(lax.rem(s + 24, 32), 2))

    barrier = pltpu.get_barrier_semaphore()
    partners = [far, sibling, *along_y, *along_x, *along_z, turn_from]
    for partner in partners:
        pl.semaphore_signal(barrier, inc=1, device_id=partner, device_id_type=MESH)
    pl.semaphore_wait(barrier, len(partners))

    def send(src, dst, send_sem, recv_sem, device):
        pltpu.make_async_remote_copy(
            src_ref=src, dst_ref=dst, send_sem=send_sem, recv_sem=recv_sem,
            device_id=device, device_id_type=MESH,
        ).start()

    own = rows((core * 8 + zh * 4 + y) * 128, 128)
    other = rows((core * 8 + (1 - zh) * 4 + y) * 128, 128)
    mine = rows(core * 1024, 1024)
    here = rows(s * 64, 64)
    column = rows(x * 512, 512)

    slots[here, :] = memory_ref[...].astype(jnp.float32).T.astype(jnp.bfloat16)
    turn_slot = rows(turn_to[0] * 64, 64)
    send(slots.at[here], feats.at[turn_slot], small_send.at[0], small_recv.at[0], turn_to)
    for device in along_z:
        send(slots.at[here], slots.at[here], small_send.at[1], small_recv.at[1], device)

    for h in range(HEADS):
        weights[h, own, :] = weight_ref[0, :, h * HD : (h + 1) * HD]

    def own_weights(h, _):
        piece = weights.at[h, own]
        send(piece, piece, w_send.at[h], w_z.at[h], far)
        for device in along_y:
            send(piece, piece, w_send.at[h], w_y.at[h], device)
        return 0

    lax.fori_loop(0, HEADS, own_weights, 0)

    wait_bytes(feats.at[pl.ds(0, 64)], small_recv.at[0])
    for device in along_z:
        send(feats.at[here], feats.at[here], small_send.at[2], small_recv.at[2], device)
    wait_bytes(slots.at[pl.ds(0, 448)], small_recv.at[1])
    for device in along_x:
        send(slots.at[column], slots.at[column], small_send.at[3], small_recv.at[3], device)

    scale_cols_one[...] = jnp.zeros((128, 128), jnp.float32)
    scale_cols_two[...] = jnp.zeros((128, 128), jnp.float32)
    scale_cols_one[0:16, :] = scales_one_ref[0]
    scale_cols_two[0:16, :] = scales_two_ref[0]
    scale_cols_one[...] = scale_cols_one[...].T
    scale_cols_two[...] = scale_cols_two[...].T
    new_cols_one[...] = jnp.zeros((128, 128), jnp.float32)
    new_cols_two[...] = jnp.zeros((128, 128), jnp.float32)
    terms[...] = jnp.zeros((2048, 128), jnp.float32)

    wait_bytes(feats.at[pl.ds(0, 448)], small_recv.at[2])
    for device in along_x:
        send(feats.at[column], feats.at[column], small_send.at[4], small_recv.at[4], device)

    wait_bytes(slots.at[pl.ds(0, 1536)], small_recv.at[3])
    for block in range(16):
        place = block_place(block)
        encoded[:, place * 128 : (place + 1) * 128] = (
            slots[block * 128 : (block + 1) * 128, :].astype(jnp.float32).T.astype(jnp.bfloat16)
        )

    def relay(buf, send_sem, z_sem, y_sem, h):
        wait_bytes(buf.at[h, pl.ds(0, 128)], z_sem.at[h])
        piece = buf.at[h, other]
        for device in along_y:
            send(piece, piece, send_sem.at[h], y_sem.at[h], device)

    def to_sibling(buf, send_sem, y_sem, core_sem, h):
        wait_bytes(buf.at[h, pl.ds(0, 768)], y_sem.at[h])
        piece = buf.at[h, mine]
        send(piece, piece, send_sem.at[h], core_sem.at[h], sibling)

    def key_gradient(h):
        wait_bytes(weights.at[h, pl.ds(0, 1024)], w_core.at[h])
        columns = rows(h * HD, HD)
        head_queries = queries_ref[0, :, columns]
        key_rows = dot(encoded[...], weights[h]).astype(jnp.bfloat16)
        expon = jnp.exp(dot(key_rows, head_queries, NT) * SCALE)
        probs = expon / jnp.sum(expon, axis=0, keepdims=True)
        prob_grad = dot(values_ref[0, :, columns], out_grad_ref[0, :, columns], NT)
        score_grad = probs * (prob_grad - jnp.sum(probs * prob_grad, axis=0, keepdims=True)) * SCALE
        key_grad = dot(score_grad.astype(jnp.bfloat16), head_queries).astype(jnp.bfloat16)
        grads[h, own, :] = key_grad
        piece = grads.at[h, own]
        send(piece, piece, g_send.at[h], g_z.at[h], far)
        for device in along_y:
            send(piece, piece, g_send.at[h], g_y.at[h], device)
        terms[...] += dot(weights[h], key_grad, NT)

    lane = lax.broadcasted_iota(jnp.int32, (128, 128), 1)

    def adam(h):
        wait_bytes(grads.at[h, pl.ds(0, 1024)], g_core.at[h])
        weight_grad = dot(feat_rows[...], grads[h])
        for part in range(HD // 128):
            block = h * (HD // 128) + part
            columns = rows(block * 128, 128)
            grad = weight_grad[:, part * 128 : (part + 1) * 128]
            chosen = lane == block
            scale_one = jnp.sum(jnp.where(chosen, scale_cols_one[...], 0.0), axis=1, keepdims=True)
            scale_two = jnp.sum(jnp.where(chosen, scale_cols_two[...], 0.0), axis=1, keepdims=True)
            first_prev = codes_one_ref[0, :, columns].astype(jnp.float32) * scale_one
            second_prev = codes_two_ref[0, :, columns].astype(jnp.float32) * scale_two
            first = beta_one * first_prev + (1.0 - beta_one) * grad
            second = beta_two * second_prev + (1.0 - beta_two) * grad * grad
            update = first / corr_one / (jnp.sqrt(second / corr_two) + 1e-08)
            first_max = jnp.max(jnp.abs(first), axis=1, keepdims=True) + 1e-06
            second_max = jnp.max(second, axis=1, keepdims=True) + 1e-06
            update_ref[0, :, columns] = update.astype(jnp.bfloat16)
            new_one_ref[0, :, columns] = (first / first_max).astype(jnp.bfloat16)
            new_two_ref[0, :, columns] = (second / second_max).astype(jnp.bfloat16)
            new_cols_one[...] = jnp.where(chosen, first_max, new_cols_one[...])
            new_cols_two[...] = jnp.where(chosen, second_max, new_cols_two[...])

    def memory_terms():
        for block in range(16):
            place = block_place(block)
            halves_out[block * 128 : (block + 1) * 128, :] = (
                terms[place * 128 : (place + 1) * 128, :].astype(jnp.bfloat16)
            )
        for k, device in zip((1, 3, 2), along_x):
            part = rows(lax.rem(x + k, 4) * 512, 512)
            send(halves_out.at[part], halves_in.at[k - 1], small_send.at[5], small_recv.at[5], device)

        wait_bytes(feats.at[pl.ds(0, 1536)], small_recv.at[4])
        for block in range(16):
            place = block_place(block)
            at = ((block + 4) % 16) * 128
            feat_rows[:, place * 128 : (place + 1) * 128] = feats[at : at + 128, :]

    def memory_columns():
        wait_bytes(halves_out.at[pl.ds(0, 1536)], small_recv.at[5])
        total = halves_out[column, :].astype(jnp.float32)
        for k in range(3):
            total += halves_in[k].astype(jnp.float32)
        parts_out[...] = total.astype(jnp.bfloat16)
        for k, device in zip(range(1, 8), along_z):
            part = rows(lax.rem(zl + k, 8) * 64, 64)
            send(parts_out.at[part], parts_in.at[k - 1], small_send.at[6], small_recv.at[6], device)

    def memory_result():
        wait_bytes(parts_out.at[pl.ds(0, 448)], small_recv.at[6])
        total = parts_out[rows(zl * 64, 64), :].astype(jnp.float32)
        for k in range(7):
            total += parts_in[k].astype(jnp.float32)
        memory_grad_ref[...] = total

    def step(t, _):
        @pl.when(t < HEADS)
        def _():
            relay(weights, w_send, w_z, w_y, t)

        @pl.when((t >= 1) & (t < HEADS + 1))
        def _():
            to_sibling(weights, w_send, w_y, w_core, t - 1)

        @pl.when((t >= 2) & (t < HEADS + 2))
        def _():
            key_gradient(t - 2)

        @pl.when(t == HEADS + 1)
        def _():
            memory_terms()

        @pl.when(t == HEADS + 3)
        def _():
            memory_columns()

        @pl.when(t == HEADS + 6)
        def _():
            memory_result()

        u = t - GRAD_LAG

        @pl.when((u >= 0) & (u < HEADS))
        def _():
            relay(grads, g_send, g_z, g_y, u)

        @pl.when((u >= 1) & (u < HEADS + 1))
        def _():
            to_sibling(grads, g_send, g_y, g_core, u - 1)

        @pl.when((u >= 2) & (u < HEADS + 2))
        def _():
            adam(u - 2)

        return 0

    lax.fori_loop(0, GRAD_LAG + HEADS + 2, step, 0)
    new_scale_one_ref[0] = new_cols_one[...].T[0:16, :]
    new_scale_two_ref[0] = new_cols_two[...].T[0:16, :]

    def sent(h, _):
        wait_bytes(weights.at[h, pl.ds(0, 1920)], w_send.at[h])
        wait_bytes(grads.at[h, pl.ds(0, 1920)], g_send.at[h])
        return 0

    lax.fori_loop(0, HEADS, sent, 0)
    for k, count in enumerate((64, 448, 448, 1536, 1536, 1536, 448)):
        wait_bytes(slots.at[pl.ds(0, count)], small_send.at[k])


def local(memory, queries, values, out_grad, key_weight, codes_one, scales_one, codes_two, scales_two):
    bf16, f32 = jnp.bfloat16, jnp.float32
    vmem = pl.BlockSpec(memory_space=pltpu.VMEM)
    sems = pltpu.SemaphoreType.DMA
    outs = pl.pallas_call(
        kernel,
        out_shape=(
            jax.ShapeDtypeStruct((64, 128), f32),
            jax.ShapeDtypeStruct((1, 128, 2048), bf16),
            jax.ShapeDtypeStruct((1, 128, 2048), bf16),
            jax.ShapeDtypeStruct((1, 16, 128), f32),
            jax.ShapeDtypeStruct((1, 128, 2048), bf16),
            jax.ShapeDtypeStruct((1, 16, 128), f32),
        ),
        in_specs=[vmem] * 9,
        out_specs=(vmem,) * 6,
        scratch_shapes=[
            pltpu.VMEM((HEADS, 2048, HD), bf16),
            pltpu.VMEM((HEADS, 2048, HD), bf16),
            pltpu.VMEM((2048, 128), bf16),
            pltpu.VMEM((2048, 128), bf16),
            pltpu.VMEM((128, 2048), bf16),
            pltpu.VMEM((128, 2048), bf16),
            pltpu.VMEM((2048, 128), f32),
            pltpu.VMEM((2048, 128), bf16),
            pltpu.VMEM((3, 512, 128), bf16),
            pltpu.VMEM((512, 128), bf16),
            pltpu.VMEM((7, 64, 128), bf16),
            pltpu.VMEM((128, 128), f32),
            pltpu.VMEM((128, 128), f32),
            pltpu.VMEM((128, 128), f32),
            pltpu.VMEM((128, 128), f32),
            sems((7,)),
            sems((7,)),
        ]
        + [sems((HEADS,))] * 8,
        compiler_params=pltpu.CompilerParams(
            collective_id=0, has_side_effects=True, vmem_limit_bytes=48 << 20
        ),
        name="projection_backward",
    )(memory, queries, values, out_grad, key_weight, codes_one, scales_one, codes_two, scales_two)
    return (outs[0].T, *outs[1:])


def solution(mesh):
    return jax.shard_map(
        local,
        mesh=mesh,
        in_specs=(
            P("dp", "section"),
            P("section", "dp", None),
            P("section", "dp", None),
            P("section", "dp", None),
            P("section", "dp", None),
            P("section", "dp", None),
            P("section", None, "dp"),
            P("section", "dp", None),
            P("section", None, "dp"),
        ),
        out_specs=(
            P("dp", "section"),
            P("section", "dp", None),
            P("section", "dp", None),
            P("section", None, "dp"),
            P("section", "dp", None),
            P("section", None, "dp"),
        ),
        check_vma=False,
    )
```

time: 650 us -> 167 us (0.26)
  the two profiles are of different devices: /device:TPU:16 before, /device:TPU:6 now
where the time goes in v1:
time: 167 us; the launch traced here: 165 us
  Pallas kernels  153 us (92%)
  local copies, waits for them, and re-layouts  11.3 us (7%)
    pallas_call x1, Pallas kernels, local(): pl.pallas_call(kernel, out_shape=(jax.ShapeDtypeStruct((64, 128), f32), j...  153 us
    unnamed x23, local copies, waits for them, and re-layouts  11.3 us

profile of v1, /device:TPU:6, one launch (start us, length us, event | category | flops | bytes accessed | tf_op | source)
XLA Modules:
  0.0 164.8 jit_solution(2118255356705560781)
XLA Ops:
  0.6 0.0 copy-start.7
  0.6 0.0 copy-start.6
  0.7 0.8 copy.15.memory_ref
  1.5 0.0 copy-done.7
  1.5 0.0 copy-done.6
  1.5 0.0 copy-start
  1.5 1.0 copy-done
  2.6 0.0 copy-start.1
  2.6 1.0 copy-done.1
  3.6 0.0 copy-start.2
  3.6 1.0 copy-done.2
  4.6 0.0 copy-start.3
  4.6 1.0 copy-done.3
  5.7 0.0 copy-start.4
  5.7 1.0 copy-done.4
  6.7 0.0 copy-start.5
  6.7 1.0 copy-done.5
  7.8 152.9 %projection_backward.1 = (f32[64,128]{1,0:T(8,128)S(1)}, bf16[1,128,2048]{2,1,0:T(8,128)(2,1)S(1)}, bf16[1,128,2048]{2,1,0:T(8,128)(2,1)S(1)}, f32[1,16,128]{2,1...) custom-call(bf16[128,64]{1,0:T(8,128)(2,1)S(1)} %copy.15.memory_ref, ...), custom_call_target="tpu_custom_call" | custom-call | tf_op jit(solution)/shard_map/projection_backward/pallas_call | solution.py:271
  160.6 0.6 copy.22
  161.2 0.8 copy.23
  162.0 0.8 copy.24
  162.8 0.6 copy.25
  163.4 0.8 copy.26
  164.2 0.6 copy.27
Async XLA Ops:
  0.6 0.9 copy-start.7
  0.6 0.9 copy-start.6
  1.5 1.0 copy-start
  2.6 1.0 copy-start.1
  3.6 1.0 copy-start.2
  4.6 1.0 copy-start.3
  5.7 1.0 copy-start.4
  6.7 1.0 copy-start.5

commit v2 on v1

v2 whole, which is shorter than its diff:
```python
import functools

import jax
import jax.numpy as jnp
from jax import lax
from jax.experimental import pallas as pl
from jax.experimental.pallas import tpu as pltpu
from jax.sharding import PartitionSpec as P

HEADS = 8
HD = 256
SCALE = HD ** (-0.5)
MESH = pl.DeviceIdType.MESH

beta_one = 0.9
beta_two = 0.95
corr_one = 1.0 - 0.9**10
corr_two = 1.0 - 0.95**10

GRAD_LAG = 8
FIRST, SECOND, THIRD, OWN_AHEAD = 8, 8, 8, 8
KEY_LAG = 3
NT = (((1,), (1,)), ((), ()))
NN = (((1,), (0,)), ((), ()))


def dot(a, b, dims=NN):
    return lax.dot_general(a, b, dims, preferred_element_type=jnp.float32)


def block_place(q):
    return (q % 2) * 8 + (q // 8) * 4 + (q // 2) % 4


def reversed_bits(z):
    return (z % 2) * 4 + z // 2 % 2 * 2 + z // 4


def rows(start, size):
    return pl.ds(pl.multiple_of(start, size), size)


def wait_bytes(ref, sem):
    pltpu.make_async_copy(ref, ref, sem).wait()


def writer(*refs):
    count = len(refs) // 2
    sem = refs[-1]
    copies = [pltpu.make_async_copy(refs[k], refs[count + k], sem.at[k]) for k in range(count)]
    for copy in copies:
        copy.start()
    for copy in copies:
        copy.wait()


def kernel(
    memory_hbm, queries_hbm, values_hbm, out_grad_hbm, weight_hbm,
    codes_one_hbm, scales_one_ref, codes_two_hbm, scales_two_ref,
    memory_grad_ref, update_ref, new_one_ref, new_scale_one_ref, new_two_ref, new_scale_two_ref,
    queries_ref, values_ref, out_grad_ref, codes_one_ref, codes_two_ref,
    weights, grads, slots, feats, encoded, feat_rows, terms, halves_out, halves_in, totals, parts_out, parts_in,
    scale_cols_one, scale_cols_two, new_cols_one, new_cols_two,
    load_sem, turn_send, turn_recv, column_send, column_recv, x_send, x_recv,
    half_send, half_recv, part_send, part_recv,
    wo_send, wo_behind, w_send, w_z, w_behind, w_rest, w_core,
    g_send, go_behind, go_rest, go_core, g_z, g_behind, g_rest, g_core,
):
    s = lax.axis_index("section")
    q = lax.axis_index("dp")
    x, zl = lax.div(s, 8), lax.rem(s, 8)
    zh, y, core = lax.div(q, 8), lax.rem(lax.div(q, 2), 4), lax.rem(q, 2)
    y_ahead, y_behind = lax.rem(y + 5 - 2 * core, 4), lax.rem(y + 3 + 2 * core, 4)

    far = (s, lax.rem(q + 8, 16))
    sibling = (s, q + 1 - 2 * core)
    ahead = (s, zh * 8 + y_ahead * 2 + core)
    behind = (s, zh * 8 + y_behind * 2 + core)
    along_x = [(lax.rem(s + 8 * k, 32), q) for k in (1, 3, 2)]
    half_bit, quarter_bit, unit_bit = lax.div(zl, 4), lax.rem(lax.div(zl, 2), 2), lax.rem(zl, 2)
    pairs = [(s + 4 - 8 * half_bit, q), (s + 2 - 4 * quarter_bit, q), (s + 1 - 2 * unit_bit, q)]
    turn_to = (lax.rem(2 * q + lax.rem(s, 2) + 8, 32), lax.div(s, 2))
    turn_from = (2 * q + lax.rem(s, 2), lax.div(lax.rem(s + 24, 32), 2))

    first_half, second_half = core * 8 + zh * 4, core * 8 + (1 - zh) * 4
    own, own_behind = rows((first_half + y) * 128, 128), rows((first_half + y_behind) * 128, 128)
    other, other_behind = rows((second_half + y) * 128, 128), rows((second_half + y_behind) * 128, 128)
    mine = rows(core * 1024, 1024)
    own_half, other_half = rows(first_half * 128, 512), rows(second_half * 128, 512)
    column = rows(x * 512, 512)
    place = unit_bit * 4 + quarter_bit * 2 + half_bit
    groups = [rows((x * 8 + place) * 64, 64), rows((x * 4 + lax.div(place, 2)) * 128, 128), rows((x * 2 + unit_bit) * 256, 256)]
    here = groups[0]

    load_memory = pltpu.make_async_copy(memory_hbm, slots.at[here], load_sem.at[0])
    load_memory.start()

    def load_weight(h):
        return pltpu.make_async_copy(
            weight_hbm.at[0, :, h * HD : (h + 1) * HD], weights.at[h, own], load_sem.at[6 + h]
        )

    for h in range(HEADS):
        load_weight(h).start()
    loads = [
        pltpu.make_async_copy(src, dst, load_sem.at[1 + k])
        for k, (src, dst) in enumerate(
            (
                (queries_hbm, queries_ref), (values_hbm, values_ref), (out_grad_hbm, out_grad_ref),
                (codes_one_hbm, codes_one_ref), (codes_two_hbm, codes_two_ref),
            )
        )
    ]
    for load in loads:
        load.start()

    barrier = pltpu.get_barrier_semaphore()
    partners = [far, sibling, ahead, behind, *along_x, *pairs, turn_from]
    for partner in partners:
        pl.semaphore_signal(barrier, inc=1, device_id=partner, device_id_type=MESH)
    pl.semaphore_wait(barrier, len(partners))

    def send(src, dst, send_sem, recv_sem, device):
        pltpu.make_async_remote_copy(
            src_ref=src, dst_ref=dst, send_sem=send_sem, recv_sem=recv_sem,
            device_id=device, device_id_type=MESH,
        ).start()

    load_memory.wait()

    def along_z(buf, base, k):
        piece = buf.at[groups[k]]
        send(piece, piece, column_send.at[base + k], column_recv.at[base + k], pairs[k])

    def along_z_next(buf, base, k):
        wait_bytes(buf.at[pl.ds(0, 64 << (k - 1))], column_recv.at[base + k - 1])
        along_z(buf, base, k)

    along_z(slots, 0, 0)
    send(slots.at[here], feats.at[rows((lax.div(turn_to[0], 8) * 8 + reversed_bits(lax.rem(turn_to[0], 8))) * 64, 64)], turn_send.at[0], turn_recv.at[0], turn_to)

    def weight_columns():
        wait_bytes(feats.at[pl.ds(0, 64)], turn_recv.at[0])
        along_z(feats, 3, 0)

    def far_weights(h):
        columns = rows(h * HD, HD)
        send(weight_hbm.at[0, :, columns], weights.at[h, own], w_send.at[h], w_z.at[h], far)

    def spread(buf, piece, send_sem, behind_sem, rest_sem, h):
        piece = buf.at[h, piece]
        send(piece, piece, send_sem.at[h], behind_sem.at[h], ahead)
        send(piece, piece, send_sem.at[h], rest_sem.at[h], behind)

    def own_weights(h):
        spread(weights, own, wo_send, wo_behind, w_rest, h)

    def columns_across(buf, base, k):
        wait_bytes(buf.at[pl.ds(0, 256)], column_recv.at[base + 2])
        for device in along_x:
            send(buf.at[column], buf.at[column], x_send.at[k], x_recv.at[k], device)

    along_z_next(slots, 0, 1)
    for h in range(FIRST):
        far_weights(h)
    weight_columns()
    for h in range(HEADS):
        load_weight(h).wait()
    for h in range(OWN_AHEAD):
        own_weights(h)
    for h in range(FIRST, SECOND):
        far_weights(h)

    def section_block(buf, section):
        low = (section // 8 * 8 + reversed_bits(section % 8)) * 64
        return buf[low : low + 64, :]

    def weight_features():
        wait_bytes(feats.at[pl.ds(0, 1536)], x_recv.at[1])
        for block in range(16):
            place = block_place(block)
            for half in range(2):
                feat_rows[half * 64 : (half + 1) * 64, place * 128 : (place + 1) * 128] = section_block(
                    feats, (2 * block + half + 8) % 32
                )

    def encode():
        wait_bytes(slots.at[pl.ds(0, 1536)], x_recv.at[0])
        for block in range(16):
            place = block_place(block)
            features = jnp.concatenate([section_block(slots, 2 * block + half) for half in range(2)], axis=0)
            encoded[:, place * 128 : (place + 1) * 128] = features.astype(jnp.float32).T.astype(jnp.bfloat16)
        scale_cols_one[...] = jnp.zeros((128, 128), jnp.float32)
        scale_cols_two[...] = jnp.zeros((128, 128), jnp.float32)
        scale_cols_one[0:16, :] = scales_one_ref[0]
        scale_cols_two[0:16, :] = scales_two_ref[0]
        scale_cols_one[...] = scale_cols_one[...].T
        scale_cols_two[...] = scale_cols_two[...].T
        new_cols_one[...] = jnp.zeros((128, 128), jnp.float32)
        new_cols_two[...] = jnp.zeros((128, 128), jnp.float32)
        terms[...] = jnp.zeros((2048, 128), jnp.float32)
        for load in loads:
            load.wait()

    def relay(buf, piece, send_sem, behind_sem, rest_sem, h):
        wait_bytes(buf.at[h, pl.ds(0, 128)], behind_sem.at[h])
        piece = buf.at[h, piece]
        send(piece, piece, send_sem.at[h], rest_sem.at[h], ahead)

    def to_sibling(buf, half, count, send_sem, rest_sem, core_sem, h):
        wait_bytes(buf.at[h, pl.ds(0, count)], rest_sem.at[h])
        piece = buf.at[h, half]
        send(piece, piece, send_sem.at[h], core_sem.at[h], sibling)

    def key_gradient(h):
        wait_bytes(weights.at[h, pl.ds(0, 1024)], w_core.at[h])
        columns = rows(h * HD, HD)
        head_queries = queries_ref[0, :, columns]
        key_rows = dot(encoded[...], weights[h]).astype(jnp.bfloat16)
        expon = jnp.exp(dot(key_rows, head_queries, NT) * SCALE)
        probs = expon / jnp.sum(expon, axis=0, keepdims=True)
        prob_grad = dot(values_ref[0, :, columns], out_grad_ref[0, :, columns], NT)
        score_grad = probs * (prob_grad - jnp.sum(probs * prob_grad, axis=0, keepdims=True)) * SCALE
        key_grad = dot(score_grad.astype(jnp.bfloat16), head_queries).astype(jnp.bfloat16)
        grads[h, own, :] = key_grad
        piece = grads.at[h, own]
        send(piece, piece, g_send.at[h], g_z.at[h], far)
        spread(grads, own, g_send, go_behind, go_rest, h)
        terms[...] += dot(weights[h], key_grad, NT)

    lane = lax.broadcasted_iota(jnp.int32, (128, 128), 1)

    def adam(h):
        wait_bytes(grads.at[h, pl.ds(0, 512)], go_core.at[h])
        wait_bytes(grads.at[h, pl.ds(0, 512)], g_core.at[h])
        weight_grad = dot(feat_rows[...], grads[h])
        for part in range(HD // 128):
            block = h * (HD // 128) + part
            columns = rows(block * 128, 128)
            grad = weight_grad[:, part * 128 : (part + 1) * 128]
            chosen = lane == block
            scale_one = jnp.sum(jnp.where(chosen, scale_cols_one[...], 0.0), axis=1, keepdims=True)
            scale_two = jnp.sum(jnp.where(chosen, scale_cols_two[...], 0.0), axis=1, keepdims=True)
            first_prev = codes_one_ref[0, :, columns].astype(jnp.float32) * scale_one
            second_prev = codes_two_ref[0, :, columns].astype(jnp.float32) * scale_two
            first = beta_one * first_prev + (1.0 - beta_one) * grad
            second = beta_two * second_prev + (1.0 - beta_two) * grad * grad
            update = first / corr_one / (jnp.sqrt(second / corr_two) + 1e-08)
            first_max = jnp.max(jnp.abs(first), axis=1, keepdims=True) + 1e-06
            second_max = jnp.max(second, axis=1, keepdims=True) + 1e-06
            update_ref[0, :, columns] = update.astype(jnp.bfloat16)
            new_one_ref[0, :, columns] = (first / first_max).astype(jnp.bfloat16)
            new_two_ref[0, :, columns] = (second / second_max).astype(jnp.bfloat16)
            new_cols_one[...] = jnp.where(chosen, first_max, new_cols_one[...])
            new_cols_two[...] = jnp.where(chosen, second_max, new_cols_two[...])

    def memory_terms():
        for block in range(16):
            place = block_place(block)
            halves_out[block * 128 : (block + 1) * 128, :] = (
                terms[place * 128 : (place + 1) * 128, :].astype(jnp.bfloat16)
            )
        for k, device in zip((1, 3, 2), along_x):
            part = rows(lax.rem(x + k, 4) * 512, 512)
            send(halves_out.at[part], halves_in.at[k - 1], half_send.at[0], half_recv.at[0], device)

    def exchange_parts(k):
        size = 256 >> k
        low = rows(other_blocks[k] * size, size)
        parts_out[low, :] = totals[low, :].astype(jnp.bfloat16)
        landing = parts_in.at[pl.ds(512 - 2 * size, size)]
        send(parts_out.at[low], landing, part_send.at[k], part_recv.at[k], pairs[2 - k])

    def add_parts(k):
        size = 256 >> k
        landing = pl.ds(512 - 2 * size, size)
        wait_bytes(parts_in.at[landing], part_recv.at[k])
        low = rows(kept_blocks[k] * size, size)
        totals[low, :] += parts_in[landing, :].astype(jnp.float32)

    kept_blocks = [unit_bit, unit_bit * 2 + quarter_bit, place]
    other_blocks = [1 - unit_bit, unit_bit * 2 + 1 - quarter_bit, unit_bit * 4 + quarter_bit * 2 + 1 - half_bit]

    def memory_columns():
        wait_bytes(halves_out.at[pl.ds(0, 1536)], half_recv.at[0])
        total = halves_out[column, :].astype(jnp.float32)
        for k in range(3):
            total += halves_in[k].astype(jnp.float32)
        for z in range(8):
            low = reversed_bits(z) * 64
            totals[low : low + 64, :] = total[z * 64 : (z + 1) * 64, :]
        exchange_parts(0)

    def memory_parts(k):
        add_parts(k)
        exchange_parts(k + 1)

    def memory_result():
        add_parts(2)
        memory_grad_ref[...] = totals[rows(place * 64, 64), :]

    def far_range(first, last):
        for h in range(first, last):
            far_weights(h)

    def step(t, _):
        def at(first, count, act):
            @pl.when((t >= first) & (t < first + count))
            def _():
                act(t - first)

        k, g = KEY_LAG, GRAD_LAG
        at(0, HEADS, lambda h: spread_far(weights, w_send, w_z, w_behind, w_rest, h))
        at(0, HEADS - OWN_AHEAD, lambda h: own_weights(h + OWN_AHEAD))
        at(0, 1, lambda h: along_z_next(slots, 0, 2))
        at(0, 1, lambda h: along_z_next(feats, 3, 1))
        at(0, 1, lambda h: far_range(SECOND, THIRD))
        at(1, 1, lambda h: columns_across(slots, 0, 0))
        at(1, 1, lambda h: along_z_next(feats, 3, 2))
        at(1, 1, lambda h: far_range(THIRD, HEADS))
        at(2, 1, lambda h: columns_across(feats, 3, 1))
        at(0, HEADS, lambda h: relay(weights, own_behind, w_send, wo_behind, w_rest, h))
        at(1, HEADS, lambda h: relay(weights, other_behind, w_send, w_behind, w_rest, h))
        at(2, HEADS, lambda h: to_sibling(weights, mine, 512, w_send, w_rest, w_core, h))
        at(k, 1, lambda h: encode())
        at(k, HEADS, key_gradient)
        at(k + HEADS - 1, 1, lambda h: memory_terms())
        at(k + 1, HEADS, lambda h: relay(grads, own_behind, g_send, go_behind, go_rest, h))
        at(k + 2, HEADS, lambda h: to_sibling(grads, own_half, 256, g_send, go_rest, go_core, h))
        at(g, HEADS, lambda h: spread_far(grads, g_send, g_z, g_behind, g_rest, h))
        at(g + 1, HEADS, lambda h: relay(grads, other_behind, g_send, g_behind, g_rest, h))
        at(g + 2, HEADS, lambda h: to_sibling(grads, other_half, 256, g_send, g_rest, g_core, h))
        at(g + 3, 1, lambda h: weight_features())
        at(g + 3, HEADS, adam)
        at(k + HEADS + 1, 1, lambda h: memory_columns())
        at(k + HEADS + 2, 1, lambda h: memory_parts(0))
        at(k + HEADS + 3, 1, lambda h: memory_parts(1))
        at(k + HEADS + 4, 1, lambda h: memory_result())
        return 0

    def spread_far(buf, send_sem, z_sem, behind_sem, rest_sem, h):
        wait_bytes(buf.at[h, pl.ds(0, 128)], z_sem.at[h])
        spread(buf, other, send_sem, behind_sem, rest_sem, h)

    lax.fori_loop(0, GRAD_LAG + HEADS + 3, step, 0)
    new_scale_one_ref[0] = new_cols_one[...].T[0:16, :]
    new_scale_two_ref[0] = new_cols_two[...].T[0:16, :]

    def sent(h, _):
        wait_bytes(weights.at[h, pl.ds(0, 1664)], w_send.at[h])
        wait_bytes(weights.at[h, pl.ds(0, 256)], wo_send.at[h])
        wait_bytes(grads.at[h, pl.ds(0, 1920)], g_send.at[h])
        return 0

    lax.fori_loop(0, HEADS, sent, 0)
    wait_bytes(slots.at[pl.ds(0, 64)], turn_send.at[0])
    wait_bytes(slots.at[pl.ds(0, 1536)], x_send.at[0])
    wait_bytes(slots.at[pl.ds(0, 1536)], x_send.at[1])
    for k in range(3):
        wait_bytes(slots.at[pl.ds(0, 64 << k)], column_send.at[k])
        wait_bytes(slots.at[pl.ds(0, 64 << k)], column_send.at[3 + k])
        wait_bytes(parts_out.at[pl.ds(0, 256 >> k)], part_send.at[k])
    wait_bytes(halves_out.at[pl.ds(0, 1536)], half_send.at[0])


def local(memory, queries, values, out_grad, key_weight, codes_one, scales_one, codes_two, scales_two):
    bf16, f32 = jnp.bfloat16, jnp.float32
    vmem, anywhere = pl.BlockSpec(memory_space=pltpu.VMEM), pl.BlockSpec(memory_space=pl.ANY)
    sems = pltpu.SemaphoreType.DMA
    one, each = sems((1,)), sems((HEADS,))
    shapes = (
        jax.ShapeDtypeStruct((64, 128), f32),
        jax.ShapeDtypeStruct((1, 128, 2048), bf16),
        jax.ShapeDtypeStruct((1, 128, 2048), bf16),
        jax.ShapeDtypeStruct((1, 16, 128), f32),
        jax.ShapeDtypeStruct((1, 128, 2048), bf16),
        jax.ShapeDtypeStruct((1, 16, 128), f32),
    )
    outs = pl.pallas_call(
        kernel,
        out_shape=shapes,
        in_specs=[anywhere] * 6 + [vmem, anywhere, vmem],
        out_specs=(vmem,) * 6,
        scratch_shapes=[pltpu.VMEM((1, 128, 2048), bf16)] * 5
        + [
            pltpu.VMEM((HEADS, 2048, HD), bf16),
            pltpu.VMEM((HEADS, 2048, HD), bf16),
            pltpu.VMEM((2048, 128), bf16),
            pltpu.VMEM((2048, 128), bf16),
            pltpu.VMEM((128, 2048), bf16),
            pltpu.VMEM((128, 2048), bf16),
            pltpu.VMEM((2048, 128), f32),
            pltpu.VMEM((2048, 128), bf16),
            pltpu.VMEM((3, 512, 128), bf16),
            pltpu.VMEM((512, 128), f32),
            pltpu.VMEM((512, 128), bf16),
            pltpu.VMEM((512, 128), bf16),
        ]
        + [pltpu.VMEM((128, 128), f32)] * 4
        + [sems((6 + HEADS,)), one, one, sems((6,)), sems((6,)), sems((2,)), sems((2,)), one, one, sems((3,)), sems((3,))]
        + [each] * 7
        + [each] * 8,
        compiler_params=pltpu.CompilerParams(
            collective_id=0, has_side_effects=True, vmem_limit_bytes=56 << 20
        ),
        name="projection_backward",
    )(memory.T, queries, values, out_grad, key_weight, codes_one, scales_one, codes_two, scales_two)
    outs = pl.pallas_call(
        writer,
        out_shape=shapes,
        in_specs=[vmem] * 6,
        out_specs=(anywhere,) * 6,
        scratch_shapes=[sems((6,))],
        name="write_results",
    )(*outs)
    return (outs[0].T, *outs[1:])


def solution(mesh):
    return jax.shard_map(
        local,
        mesh=mesh,
        in_specs=(
            P("dp", "section"),
            P("section", "dp", None),
            P("section", "dp", None),
            P("section", "dp", None),
            P("section", "dp", None),
            P("section", "dp", None),
            P("section", None, "dp"),
            P("section", "dp", None),
            P("section", None, "dp"),
        ),
        out_specs=(
            P("dp", "section"),
            P("section", "dp", None),
            P("section", "dp", None),
            P("section", None, "dp"),
            P("section", "dp", None),
            P("section", None, "dp"),
        ),
        check_vma=False,
    )
```

time: 167 us -> 152 us (0.910)
  the two profiles are of different devices: /device:TPU:6 before, /device:TPU:3 now
where the time goes in v2:
time: 152 us
  Pallas kernels  151 us (99%)
    pallas_call x1, Pallas kernels, local(): pl.pallas_call(kernel, out_shape=shapes, in_specs=[anywhere] * 6 + [vmem,...  148 us

profile of v2, /device:TPU:3, one launch (start us, length us, event | category | flops | bytes accessed | tf_op | source)
XLA Modules:
  0.0 151.6 jit_solution(166182632946368498)
XLA Ops:
  0.6 148.3 %projection_backward.1 = (f32[64,128]{1,0:T(8,128)}, bf16[1,128,2048]{2,1,0:T(8,128)(2,1)}, bf16[1,128,2048]{2,1,0:T(8,128)(2,1)}, f32[1,16,128]{2,1,0:T(8,128)}...) custom-call(bf16[64,128]{1,0:T(8,128)(2,1)} %bitcast.2, bf16[1,128,2048]{2,1,0:T(8,128)(2,1)} %queries_hbm.1, ...), custom_call_target="tpu_custom_call" | custom-call | tf_op jit(solution)/shard_map/projection_backward/pallas_call | solution.py:379
  149.0 2.6 %write_results.1 = (f32[64,128]{1,0:T(8,128)}, bf16[1,128,2048]{2,1,0:T(8,128)(2,1)}, bf16[1,128,2048]{2,1,0:T(8,128)(2,1)}, f32[1,16,128]{2,1,0:T(8,128)}, bf16...) custom-call(f32[64,128]{1,0:T(8,128)} %get-tuple-element.18.refs_0_, bf16[1,128,2048]{2,1,0:T(8,128)(2,1)} %get-tuple-element.19.refs_1_, ...), custom_call_target="tpu_custom_call" | custom-call | tf_op jit(solution)/shard_map/write_results/pallas_call | solution.py:408

commit v3 on v2

--- a/solution.py
+++ b/solution.py
@@ -17,9 +17,10 @@
 corr_one = 1.0 - 0.9**10
 corr_two = 1.0 - 0.95**10
 
-GRAD_LAG = 8
+GRAD_LAG = 6
 FIRST, SECOND, THIRD, OWN_AHEAD = 8, 8, 8, 8
-KEY_LAG = 3
+KEY_LAG = 4
+FAR_LAG = 1
 NT = (((1,), (1,)), ((), ()))
 NN = (((1,), (0,)), ((), ()))
 
@@ -59,12 +60,13 @@
     codes_one_hbm, scales_one_ref, codes_two_hbm, scales_two_ref,
     memory_grad_ref, update_ref, new_one_ref, new_scale_one_ref, new_two_ref, new_scale_two_ref,
     queries_ref, values_ref, out_grad_ref, codes_one_ref, codes_two_ref,
-    weights, grads, slots, feats, encoded, feat_rows, terms, halves_out, halves_in, totals, parts_out, parts_in,
+    weights, grads, w_passing, g_passing, slots, feats, encoded, feat_rows, terms, halves_out, halves_in, totals, parts_out, parts_in,
     scale_cols_one, scale_cols_two, new_cols_one, new_cols_two,
     load_sem, turn_send, turn_recv, column_send, column_recv, x_send, x_recv,
     half_send, half_recv, part_send, part_recv,
     wo_send, wo_behind, w_send, w_z, w_behind, w_rest, w_core,
     g_send, go_behind, go_rest, go_core, g_z, g_behind, g_rest, g_core,
+    w_up, w_down, g_up, g_down,
 ):
     s = lax.axis_index("section")
     q = lax.axis_index("dp")
@@ -72,7 +74,13 @@
     zh, y, core = lax.div(q, 8), lax.rem(lax.div(q, 2), 4), lax.rem(q, 2)
     y_ahead, y_behind = lax.rem(y + 5 - 2 * core, 4), lax.rem(y + 3 + 2 * core, 4)
 
-    far = (s, lax.rem(q + 8, 16))
+    z = zh * 8 + zl
+
+    def at_z(z):
+        return (x * 8 + lax.rem(z, 8), lax.div(z, 8) * 8 + lax.rem(q, 8))
+
+    z_up, z_down = lax.rem(z + 4, 16), lax.rem(z + 12, 16)
+    up, down = at_z(z_up), at_z(z_down)
     sibling = (s, q + 1 - 2 * core)
     ahead = (s, zh * 8 + y_ahead * 2 + core)
     behind = (s, zh * 8 + y_behind * 2 + core)
@@ -86,6 +94,10 @@
     own, own_behind = rows((first_half + y) * 128, 128), rows((first_half + y_behind) * 128, 128)
     other, other_behind = rows((second_half + y) * 128, 128), rows((second_half + y_behind) * 128, 128)
     mine = rows(core * 1024, 1024)
+    own_low, own_high = rows((first_half + y) * 128, 64), rows((first_half + y) * 128 + 64, 64)
+    passing_low = rows((core * 8 + lax.div(z_down, 8) * 4 + y) * 128, 64)
+    passing_high = rows((core * 8 + lax.div(z_up, 8) * 4 + y) * 128 + 64, 64)
+    low, high = pl.ds(0, 64), pl.ds(64, 64)
     own_half, other_half = rows(first_half * 128, 512), rows(second_half * 128, 512)
     column = rows(x * 512, 512)
     place = unit_bit * 4 + quarter_bit * 2 + half_bit
@@ -115,7 +127,7 @@
         load.start()
 
     barrier = pltpu.get_barrier_semaphore()
-    partners = [far, sibling, ahead, behind, *along_x, *pairs, turn_from]
+    partners = [up, down, sibling, ahead, behind, *along_x, *pairs, turn_from]
     for partner in partners:
         pl.semaphore_signal(barrier, inc=1, device_id=partner, device_id_type=MESH)
     pl.semaphore_wait(barrier, len(partners))
@@ -145,7 +157,17 @@
 
     def far_weights(h):
         columns = rows(h * HD, HD)
-        send(weight_hbm.at[0, :, columns], weights.at[h, own], w_send.at[h], w_z.at[h], far)
+        send(weight_hbm.at[0, low, columns], w_passing.at[h, low], w_send.at[h], w_up.at[h], up)
+        send(weight_hbm.at[0, high, columns], w_passing.at[h, high], w_send.at[h], w_down.at[h], down)
+
+    def pass_on(buf, passing, send_sem, up_sem, down_sem, z_sem, h):
+        wait_bytes(passing.at[h, low], up_sem.at[h])
+        send(passing.at[h, low], buf.at[h, passing_low], send_sem.at[h], z_sem.at[h], up)
+        wait_bytes(passing.at[h, high], down_sem.at[h])
+        send(passing.at[h, high], buf.at[h, passing_high], send_sem.at[h], z_sem.at[h], down)
+
+    def pass_weights(h):
+        pass_on(weights, w_passing, w_send, w_up, w_down, w_z, h)
 
     def spread(buf, piece, send_sem, behind_sem, rest_sem, h):
         piece = buf.at[h, piece]
@@ -163,7 +185,6 @@
     along_z_next(slots, 0, 1)
     for h in range(FIRST):
         far_weights(h)
-    weight_columns()
     for h in range(HEADS):
         load_weight(h).wait()
     for h in range(OWN_AHEAD):
@@ -223,8 +244,8 @@
         score_grad = probs * (prob_grad - jnp.sum(probs * prob_grad, axis=0, keepdims=True)) * SCALE
         key_grad = dot(score_grad.astype(jnp.bfloat16), head_queries).astype(jnp.bfloat16)
         grads[h, own, :] = key_grad
-        piece = grads.at[h, own]
-        send(piece, piece, g_send.at[h], g_z.at[h], far)
+        send(grads.at[h, own_low], g_passing.at[h, low], g_send.at[h], g_up.at[h], up)
+        send(grads.at[h, own_high], g_passing.at[h, high], g_send.at[h], g_down.at[h], down)
         spread(grads, own, g_send, go_behind, go_rest, h)
         terms[...] += dot(weights[h], key_grad, NT)
 
@@ -310,28 +331,32 @@
                 act(t - first)
 
         k, g = KEY_LAG, GRAD_LAG
-        at(0, HEADS, lambda h: spread_far(weights, w_send, w_z, w_behind, w_rest, h))
+        f = FAR_LAG
+        at(0, HEADS - 2, lambda h: pass_weights(h + 2))
+        at(g, HEADS, lambda h: pass_on(grads, g_passing, g_send, g_up, g_down, g_z, h))
+        at(f, HEADS, lambda h: spread_far(weights, w_send, w_z, w_behind, w_rest, h))
         at(0, HEADS - OWN_AHEAD, lambda h: own_weights(h + OWN_AHEAD))
         at(0, 1, lambda h: along_z_next(slots, 0, 2))
-        at(0, 1, lambda h: along_z_next(feats, 3, 1))
+        at(0, 1, lambda h: weight_columns())
+        at(2, 1, lambda h: along_z_next(feats, 3, 1))
         at(0, 1, lambda h: far_range(SECOND, THIRD))
         at(1, 1, lambda h: columns_across(slots, 0, 0))
-        at(1, 1, lambda h: along_z_next(feats, 3, 2))
+        at(4, 1, lambda h: along_z_next(feats, 3, 2))
         at(1, 1, lambda h: far_range(THIRD, HEADS))
-        at(2, 1, lambda h: columns_across(feats, 3, 1))
+        at(6, 1, lambda h: columns_across(feats, 3, 1))
         at(0, HEADS, lambda h: relay(weights, own_behind, w_send, wo_behind, w_rest, h))
-        at(1, HEADS, lambda h: relay(weights, other_behind, w_send, w_behind, w_rest, h))
-        at(2, HEADS, lambda h: to_sibling(weights, mine, 512, w_send, w_rest, w_core, h))
+        at(f + 1, HEADS, lambda h: relay(weights, other_behind, w_send, w_behind, w_rest, h))
+        at(f + 2, HEADS, lambda h: to_sibling(weights, mine, 512, w_send, w_rest, w_core, h))
         at(k, 1, lambda h: encode())
         at(k, HEADS, key_gradient)
         at(k + HEADS - 1, 1, lambda h: memory_terms())
         at(k + 1, HEADS, lambda h: relay(grads, own_behind, g_send, go_behind, go_rest, h))
         at(k + 2, HEADS, lambda h: to_sibling(grads, own_half, 256, g_send, go_rest, go_core, h))
-        at(g, HEADS, lambda h: spread_far(grads, g_send, g_z, g_behind, g_rest, h))
-        at(g + 1, HEADS, lambda h: relay(grads, other_behind, g_send, g_behind, g_rest, h))
-        at(g + 2, HEADS, lambda h: to_sibling(grads, other_half, 256, g_send, g_rest, g_core, h))
-        at(g + 3, 1, lambda h: weight_features())
-        at(g + 3, HEADS, adam)
+        at(g + f, HEADS, lambda h: spread_far(grads, g_send, g_z, g_behind, g_rest, h))
+        at(g + f + 1, HEADS, lambda h: relay(grads, other_behind, g_send, g_behind, g_rest, h))
+        at(g + f + 2, HEADS, lambda h: to_sibling(grads, other_half, 256, g_send, g_rest, g_core, h))
+        at(g + f + 3, 1, lambda h: weight_features())
+        at(g + f + 3, HEADS, adam)
         at(k + HEADS + 1, 1, lambda h: memory_columns())
         at(k + HEADS + 2, 1, lambda h: memory_parts(0))
         at(k + HEADS + 3, 1, lambda h: memory_parts(1))
@@ -342,14 +367,16 @@
         wait_bytes(buf.at[h, pl.ds(0, 128)], z_sem.at[h])
         spread(buf, other, send_sem, behind_sem, rest_sem, h)
 
-    lax.fori_loop(0, GRAD_LAG + HEADS + 3, step, 0)
+    pass_weights(0)
+    pass_weights(1)
+    lax.fori_loop(0, GRAD_LAG + FAR_LAG + HEADS + 3, step, 0)
     new_scale_one_ref[0] = new_cols_one[...].T[0:16, :]
     new_scale_two_ref[0] = new_cols_two[...].T[0:16, :]
 
     def sent(h, _):
-        wait_bytes(weights.at[h, pl.ds(0, 1664)], w_send.at[h])
+        wait_bytes(weights.at[h, pl.ds(0, 1792)], w_send.at[h])
         wait_bytes(weights.at[h, pl.ds(0, 256)], wo_send.at[h])
-        wait_bytes(grads.at[h, pl.ds(0, 1920)], g_send.at[h])
+        wait_bytes(grads.at[h, pl.ds(0, 2048)], g_send.at[h])
         return 0
 
     lax.fori_loop(0, HEADS, sent, 0)
@@ -385,6 +412,8 @@
         + [
             pltpu.VMEM((HEADS, 2048, HD), bf16),
             pltpu.VMEM((HEADS, 2048, HD), bf16),
+            pltpu.VMEM((HEADS, 128, HD), bf16),
+            pltpu.VMEM((HEADS, 128, HD), bf16),
             pltpu.VMEM((2048, 128), bf16),
             pltpu.VMEM((2048, 128), bf16),
             pltpu.VMEM((128, 2048), bf16),
@@ -399,7 +428,7 @@
         + [pltpu.VMEM((128, 128), f32)] * 4
         + [sems((6 + HEADS,)), one, one, sems((6,)), sems((6,)), sems((2,)), sems((2,)), one, one, sems((3,)), sems((3,))]
         + [each] * 7
-        + [each] * 8,
+        + [each] * 12,
         compiler_params=pltpu.CompilerParams(
             collective_id=0, has_side_effects=True, vmem_limit_bytes=56 << 20
         ),

time: 152 us -> 144 us (0.947)
  the two profiles are of different devices: /device:TPU:3 before, /device:TPU:6 now
where the time goes in v3:
time: 144 us; the launch traced here: 142 us
  Pallas kernels  141 us (98%)
    pallas_call x1, Pallas kernels, local(): pl.pallas_call(kernel, out_shape=shapes, in_specs=[anywhere] * 6 + [vmem,...  139 us

profile of v3, /device:TPU:6, one launch (start us, length us, event | category | flops | bytes accessed | tf_op | source)
XLA Modules:
  0.0 141.8 jit_solution(12147562338021500720)
XLA Ops:
  0.6 138.6 %projection_backward.1 = (f32[64,128]{1,0:T(8,128)}, bf16[1,128,2048]{2,1,0:T(8,128)(2,1)}, bf16[1,128,2048]{2,1,0:T(8,128)(2,1)}, f32[1,16,128]{2,1,0:T(8,128)}...) custom-call(bf16[64,128]{1,0:T(8,128)(2,1)} %bitcast.2, bf16[1,128,2048]{2,1,0:T(8,128)(2,1)} %queries_hbm.1, ...), custom_call_target="tpu_custom_call" | custom-call | tf_op jit(solution)/shard_map/projection_backward/pallas_call | solution.py:406
  139.2 2.6 %write_results.1 = (f32[64,128]{1,0:T(8,128)}, bf16[1,128,2048]{2,1,0:T(8,128)(2,1)}, bf16[1,128,2048]{2,1,0:T(8,128)(2,1)}, f32[1,16,128]{2,1,0:T(8,128)}, bf16...) custom-call(f32[64,128]{1,0:T(8,128)} %get-tuple-element.18.refs_0_, bf16[1,128,2048]{2,1,0:T(8,128)(2,1)} %get-tuple-element.19.refs_1_, ...), custom_call_target="tpu_custom_call" | custom-call | tf_op jit(solution)/shard_map/write_results/pallas_call | solution.py:437

commit v4 on v3

--- a/solution.py
+++ b/solution.py
@@ -65,7 +65,7 @@
     load_sem, turn_send, turn_recv, column_send, column_recv, x_send, x_recv,
     half_send, half_recv, part_send, part_recv,
     wo_send, wo_behind, w_send, w_z, w_behind, w_rest, w_core,
-    g_send, go_behind, go_rest, go_core, g_z, g_behind, g_rest, g_core,
+    g_send, go_behind, go_rest, go_core, g_z, g_rest, g_core,
     w_up, w_down, g_up, g_down,
 ):
     s = lax.axis_index("section")
@@ -84,6 +84,7 @@
     sibling = (s, q + 1 - 2 * core)
     ahead = (s, zh * 8 + y_ahead * 2 + core)
     behind = (s, zh * 8 + y_behind * 2 + core)
+    opposite = (s, zh * 8 + lax.rem(y + 2, 4) * 2 + core)
     along_x = [(lax.rem(s + 8 * k, 32), q) for k in (1, 3, 2)]
     half_bit, quarter_bit, unit_bit = lax.div(zl, 4), lax.rem(lax.div(zl, 2), 2), lax.rem(zl, 2)
     pairs = [(s + 4 - 8 * half_bit, q), (s + 2 - 4 * quarter_bit, q), (s + 1 - 2 * unit_bit, q)]
@@ -127,7 +128,7 @@
         load.start()
 
     barrier = pltpu.get_barrier_semaphore()
-    partners = [up, down, sibling, ahead, behind, *along_x, *pairs, turn_from]
+    partners = [up, down, sibling, ahead, behind, opposite, *along_x, *pairs, turn_from]
     for partner in partners:
         pl.semaphore_signal(barrier, inc=1, device_id=partner, device_id_type=MESH)
     pl.semaphore_wait(barrier, len(partners))
@@ -320,6 +321,12 @@
         add_parts(2)
         memory_grad_ref[...] = totals[rows(place * 64, 64), :]
 
+    def far_gradient(h):
+        wait_bytes(grads.at[h, pl.ds(0, 128)], g_z.at[h])
+        piece = grads.at[h, other]
+        for device in (ahead, behind, opposite):
+            send(piece, piece, g_send.at[h], g_rest.at[h], device)
+
     def far_range(first, last):
         for h in range(first, last):
             far_weights(h)
@@ -352,11 +359,10 @@
         at(k + HEADS - 1, 1, lambda h: memory_terms())
         at(k + 1, HEADS, lambda h: relay(grads, own_behind, g_send, go_behind, go_rest, h))
         at(k + 2, HEADS, lambda h: to_sibling(grads, own_half, 256, g_send, go_rest, go_core, h))
-        at(g + f, HEADS, lambda h: spread_far(grads, g_send, g_z, g_behind, g_rest, h))
-        at(g + f + 1, HEADS, lambda h: relay(grads, other_behind, g_send, g_behind, g_rest, h))
-        at(g + f + 2, HEADS, lambda h: to_sibling(grads, other_half, 256, g_send, g_rest, g_core, h))
-        at(g + f + 3, 1, lambda h: weight_features())
-        at(g + f + 3, HEADS, adam)
+        at(g + f, HEADS, far_gradient)
+        at(g + f + 1, HEADS, lambda h: to_sibling(grads, other_half, 384, g_send, g_rest, g_core, h))
+        at(g + f + 2, 1, lambda h: weight_features())
+        at(g + f + 2, HEADS, adam)
         at(k + HEADS + 1, 1, lambda h: memory_columns())
         at(k + HEADS + 2, 1, lambda h: memory_parts(0))
         at(k + HEADS + 3, 1, lambda h: memory_parts(1))
@@ -369,7 +375,7 @@
 
     pass_weights(0)
     pass_weights(1)
-    lax.fori_loop(0, GRAD_LAG + FAR_LAG + HEADS + 3, step, 0)
+    lax.fori_loop(0, GRAD_LAG + FAR_LAG + HEADS + 2, step, 0)
     new_scale_one_ref[0] = new_cols_one[...].T[0:16, :]
     new_scale_two_ref[0] = new_cols_two[...].T[0:16, :]
 
@@ -428,7 +434,7 @@
         + [pltpu.VMEM((128, 128), f32)] * 4
         + [sems((6 + HEADS,)), one, one, sems((6,)), sems((6,)), sems((2,)), sems((2,)), one, one, sems((3,)), sems((3,))]
         + [each] * 7
-        + [each] * 12,
+        + [each] * 11,
         compiler_params=pltpu.CompilerParams(
             collective_id=0, has_side_effects=True, vmem_limit_bytes=56 << 20
         ),

time: 144 us -> 149 us (1.035); the launches traced: 142 us -> 148 us
  Pallas kernels: 141 us -> 148 us
    pallas_call x1, Pallas kernels: 139 us -> 145 us  [local(): pl.pallas_call(kernel, out_shape=shapes, in_specs=[anywhere] * 6 + [vmem,...]
where the time goes in v4:
time: 149 us; the launch traced here: 148 us
  Pallas kernels  148 us (99%)
    pallas_call x1, Pallas kernels, local(): pl.pallas_call(kernel, out_shape=shapes, in_specs=[anywhere] * 6 + [vmem,...  145 us

profile of v4, /device:TPU:6, one launch (start us, length us, event | category | flops | bytes accessed | tf_op | source)
XLA Modules:
  0.0 148.4 jit_solution(16654373455692406635)
XLA Ops:
  0.6 145.2 %projection_backward.1 = (f32[64,128]{1,0:T(8,128)}, bf16[1,128,2048]{2,1,0:T(8,128)(2,1)}, bf16[1,128,2048]{2,1,0:T(8,128)(2,1)}, f32[1,16,128]{2,1,0:T(8,128)}...) custom-call(bf16[64,128]{1,0:T(8,128)(2,1)} %bitcast.2, bf16[1,128,2048]{2,1,0:T(8,128)(2,1)} %queries_hbm.1, ...), custom_call_target="tpu_custom_call" | custom-call | tf_op jit(solution)/shard_map/projection_backward/pallas_call | solution.py:412
  145.8 2.6 %write_results.1 = (f32[64,128]{1,0:T(8,128)}, bf16[1,128,2048]{2,1,0:T(8,128)(2,1)}, bf16[1,128,2048]{2,1,0:T(8,128)(2,1)}, f32[1,16,128]{2,1,0:T(8,128)}, bf16...) custom-call(f32[64,128]{1,0:T(8,128)} %get-tuple-element.18.refs_0_, bf16[1,128,2048]{2,1,0:T(8,128)(2,1)} %get-tuple-element.19.refs_1_, ...), custom_call_target="tpu_custom_call" | custom-call | tf_op jit(solution)/shard_map/write_results/pallas_call | solution.py:443
